TPU v7x, 256 devices: a whole 4x4x8 slice. The times are simulated.
256 devices in a mesh: row: 8 (over y_lo, x), col: 16 (over z, y_hi), layer: 2 (over core).
Axes of the slice: x: 4, y: 4 (y_hi: 2, y_lo: 2; y = y_hi * 2 + y_lo), z: 8, core: 2. Of those that a mesh axis runs over, the one named last changes fastest.
Arguments:
- initial: float32 [4096, 4096], P('row', 'col'), may hold values from -1.1 to 1.1
- pattern: int32 [32, 32], P('row', 'col'), may hold values from 0 to 1
- filters: int32 [2, 32, 32], P(None, 'row', 'col'), may hold values 0 or 1
Outputs:
- sign_matrix: float32 [4096, 4096], P('row', ('col', 'layer'))
All inputs are finite; a program needn't handle non-finite values. No bound on the sum of `filters` on one device may be relied on, other than what follows from the above.
Results may differ from a plain program's by a relative error of at most 0.00012.
Values sent between devices are 32-bit elements; how exact they have to be, the bound alone decides.
A program may use at most 64 MiB of HBM per device.

v0:
```python
import jax
import jax.numpy as jnp
from jax import lax
from jax.sharding import PartitionSpec as P

TILE = 128
ITERS = 2


def expand_tiles(tiles):
    values = tiles.astype(jnp.float32)
    row_tiles, col_tiles = values.shape
    spread = jnp.broadcast_to(values[:, None, :, None], (row_tiles, TILE, col_tiles, TILE))
    return spread.reshape(row_tiles * TILE, col_tiles * TILE)


def select_columns(matrix_in, layer_count, layer_id):
    row_count, col_count = matrix_in.shape
    grouped = matrix_in.reshape(row_count, col_count // (TILE * layer_count), layer_count, TILE)
    chosen = lax.dynamic_index_in_dim(grouped, layer_id, 2, keepdims=False)
    return chosen.reshape(row_count, col_count // layer_count)


def select_rows(matrix_in, layer_count, layer_id):
    row_count, col_count = matrix_in.shape
    grouped = matrix_in.reshape(row_count // (TILE * layer_count), layer_count, TILE, col_count)
    chosen = lax.dynamic_index_in_dim(grouped, layer_id, 1, keepdims=False)
    return chosen.reshape(row_count // layer_count, col_count)


def panel_product(left_part, right_rows):
    return jnp.dot(
        lax.all_gather(left_part, "col", axis=1, tiled=True),
        right_rows,
        precision=lax.Precision.HIGHEST,
        preferred_element_type=jnp.float32,
    )


def on_device(initial, pattern, filters):
    layer_count = lax.axis_size("layer")
    layer_id = lax.axis_index("layer")
    row_count, col_count = initial.shape
    matrix = initial * expand_tiles(pattern)
    for sweep in range(ITERS):
        filter_mask = expand_tiles(filters[sweep])
        left_part = select_columns(matrix, layer_count, layer_id)
        right_rows = lax.all_gather(
            select_rows(matrix, layer_count, layer_id), "row", axis=0, tiled=True
        )
        partial_value = filter_mask * panel_product(left_part, right_rows)
        square = lax.psum(partial_value, "layer")
        own_rows = select_rows(square, layer_count, layer_id)
        square_rows = lax.all_gather(own_rows, "row", axis=0, tiled=True)
        second = filter_mask * panel_product(left_part, square_rows)
        if sweep + 1 < ITERS:
            matrix = 1.5 * matrix - 0.5 * lax.psum(second, "layer")
        else:
            half_width = col_count // layer_count
            own_half = lax.psum_scatter(second, "layer", scatter_dimension=1, tiled=True)
            matrix = (
                1.5 * lax.dynamic_slice_in_dim(matrix, layer_id * half_width, half_width, 1)
                - 0.5 * own_half
            )
    return matrix


def solution(mesh):
    return jax.shard_map(
        on_device,
        mesh=mesh,
        in_specs=(P("row", "col"), P("row", "col"), P(None, "row", "col")),
        out_specs=P("row", ("col", "layer")),
        check_vma=False,
    )
```

profile of v0, /device:TPU:1, one launch (start us, length us, event | category | flops | bytes accessed | tf_op | source)
XLA Modules:
  0.0 600.4 jit_solution(2588826689430627526)
XLA Ops:
  6.5 0.7 convert_element_type.23
  7.5 1.1 bitcast_multiply_fusion
  8.7 0.7 constant_dynamic-slice_fusion.4
  9.7 1.0 constant_dynamic-slice_fusion.5
  10.9 41.3 %all-gather.9.cloned.1.call-done = f32[2048,256]{1,0:T(8,128)} async-done(((f32[256,256]{1,0:T(8,128)}), f32[2048,256]{1,0:T(8,128)}) %all-gather.9.cloned.1.call-update) | async-done | bytes 2097168 | tf_op jit(solution)/shard_map/all_gather | solution.py:48
  52.2 132.8 %all-gather.17.cloned.1.call-done = f32[512,1,1,2048]{3,2,0,1:T(1,128)} async-done(((f32[512,1,1,128]{3,2,0,1:T(1,128)}), f32[512,1,1,2048]{3,2,0,1:T(1,128)}) %all-gather.17.cloned.1.call-update) | async-done | bytes 4194320 | tf_op jit(solution)/shard_map/all_gather | solution.py:33
  185.1 7.9 %fusion.12 = f32[512,256]{1,0:T(8,128)} fusion(f32[2048,256]{1,0:T(8,128)} %all-gather.9.cloned.1.call-done, f32[512,1,1,2048]{3,2,0,1:T(1,128)} %all-gather.17.cloned.1.call-done, f32[64,8,2,128]{3,2,1,0:T(2,128)S(1)} %bitcast.51), kind=kOutput, calls=%fused_computation.12 | convolution fusion | flops 3221356544 | bytes 7340032 | tf_op jit(solution)/shard_map/dot_general | solution.py:32
  193.2 32.1 %all-reduce.4.cloned.1.call-done = f32[2,2,128,256]{3,2,1,0:T(8,128)} async-done(((f32[2,2,128,256]{3,2,1,0:T(8,128)}), f32[2,2,128,256]{3,2,1,0:T(8,128)}) %all-reduce.4.cloned.1.call-update) | async-done | bytes 524304 | tf_op jit(solution)/shard_map/psum | solution.py:52
  225.3 1.7 constant_dynamic-slice_fusion.3
  227.0 39.5 %all-gather.11.cloned.1.call-done = f32[2048,256]{1,0:T(8,128)} async-done(((f32[256,256]{1,0:T(8,128)}), f32[2048,256]{1,0:T(8,128)}) %all-gather.11.cloned.1.call-update) | async-done | bytes 2097168 | tf_op jit(solution)/shard_map/all_gather | solution.py:54
  266.5 7.9 %fusion.15 = f32[512,256]{1,0:T(8,128)} fusion(f32[2048,256]{1,0:T(8,128)} %all-gather.11.cloned.1.call-done, f32[512,1,1,2048]{3,2,0,1:T(1,128)} %all-gather.17.cloned.1.call-done, f32[64,8,2,128]{3,2,1,0:T(2,128)S(1)} %bitcast.52), kind=kOutput, calls=%fused_computation.13 | convolution fusion | flops 3221356544 | bytes 7340032 | tf_op jit(solution)/shard_map/dot_general | solution.py:32
  274.5 34.9 %all-reduce.6.cloned.1.call-done = f32[512,256]{1,0:T(8,128)} async-done(((f32[512,256]{1,0:T(8,128)}), f32[512,256]{1,0:T(8,128)}) %all-reduce.6.cloned.1.call-update) | async-done | bytes 524304 | tf_op jit(solution)/shard_map/psum | solution.py:57
  309.4 1.1 multiply_subtract_fusion
  310.5 0.7 constant_dynamic-slice_fusion.1
  311.6 1.0 constant_dynamic-slice_fusion.2
  312.9 37.9 %all-gather.13.cloned.1.call-done = f32[2048,256]{1,0:T(8,128)} async-done(((f32[256,256]{1,0:T(8,128)}), f32[2048,256]{1,0:T(8,128)}) %all-gather.13.cloned.1.call-update) | async-done | bytes 2097168 | tf_op jit(solution)/shard_map/all_gather | solution.py:48
  350.8 132.8 %all-gather.19.cloned.1.call-done = f32[512,1,1,2048]{3,2,0,1:T(1,128)} async-done(((f32[512,1,1,128]{3,2,0,1:T(1,128)}), f32[512,1,1,2048]{3,2,0,1:T(1,128)}) %all-gather.19.cloned.1.call-update) | async-done | bytes 4194320 | tf_op jit(solution)/shard_map/all_gather | solution.py:33
  483.8 7.9 %fusion.18 = f32[512,256]{1,0:T(8,128)} fusion(f32[2048,256]{1,0:T(8,128)} %all-gather.13.cloned.1.call-done, f32[512,1,1,2048]{3,2,0,1:T(1,128)} %all-gather.19.cloned.1.call-done, f32[64,8,2,128]{3,2,1,0:T(2,128)S(1)} %bitcast.49), kind=kOutput, calls=%fused_computation.14 | convolution fusion | flops 3221356544 | bytes 7340032 | tf_op jit(solution)/shard_map/dot_general | solution.py:32
  491.8 32.1 %all-reduce.8.cloned.1.call-done = f32[2,2,128,256]{3,2,1,0:T(8,128)} async-done(((f32[2,2,128,256]{3,2,1,0:T(8,128)}), f32[2,2,128,256]{3,2,1,0:T(8,128)}) %all-reduce.8.cloned.1.call-update) | async-done | bytes 524304 | tf_op jit(solution)/shard_map/psum | solution.py:52
  523.9 1.7 constant_dynamic-slice_fusion
  525.6 39.6 %all-gather.15.cloned.1.call-done = f32[2048,256]{1,0:T(8,128)} async-done(((f32[256,256]{1,0:T(8,128)}), f32[2048,256]{1,0:T(8,128)}) %all-gather.15.cloned.1.call-update) | async-done | bytes 2097168 | tf_op jit(solution)/shard_map/all_gather | solution.py:54
  565.2 7.9 %fusion.21 = f32[512,256]{1,0:T(8,128)} fusion(f32[2048,256]{1,0:T(8,128)} %all-gather.15.cloned.1.call-done, f32[512,1,1,2048]{3,2,0,1:T(1,128)} %all-gather.19.cloned.1.call-done, f32[64,8,2,128]{3,2,1,0:T(2,128)S(1)} %bitcast.50), kind=kOutput, calls=%fused_computation.15 | convolution fusion | flops 3221356544 | bytes 7340032 | tf_op jit(solution)/shard_map/dot_general | solution.py:32
  573.2 18.7 %reduce-scatter.2.cloned.1.call-done = f32[512,128]{1,0:T(8,128)} async-done(((f32[512,256]{1,0:T(8,128)}), f32[512,128]{1,0:T(8,128)}) %reduce-scatter.2.cloned.1.call-update) | async-done | bytes 262160 | tf_op jit(solution)/shard_map/reduce_scatter | solution.py:60
  591.9 1.7 multiply_subtract_fusion.1
  (31 shorter events, 2.2 us)
Async XLA Ops:
  6.5 4.2 copy-start
  6.5 45.6 %all-gather.9.cloned.1.call-start = ((), (), s32[]{:S(2)}) async-start(), calls=%async_computation.1 | async-start | bytes 2359296 | tf_op jit(solution)/shard_map/all_gather | solution.py:48
  9.4 175.5 %all-gather.17.cloned.1.call-start = ((), (), s32[]{:S(2)}) async-start(), calls=%async_computation.9 | async-start | bytes 4456448 | tf_op jit(solution)/shard_map/all_gather | solution.py:33
  10.7 214.6 %all-reduce.4.cloned.1.call-start = ((), (), s32[]{:S(2)}) async-start(), calls=%async_computation.2 | async-start | bytes 1048576 | tf_op jit(solution)/shard_map/psum | solution.py:52
  193.1 73.4 %all-gather.11.cloned.1.call-start = ((), (), s32[]{:S(2)}) async-start(), calls=%async_computation.3 | async-start | bytes 2359296 | tf_op jit(solution)/shard_map/all_gather | solution.py:54
  227.0 82.4 %all-reduce.6.cloned.1.call-start = ((), (), s32[]{:S(2)}) async-start(), calls=%async_computation.4 | async-start | bytes 1048576 | tf_op jit(solution)/shard_map/psum | solution.py:57
  274.5 76.3 %all-gather.13.cloned.1.call-start = ((), (), s32[]{:S(2)}) async-start(), calls=%async_computation.5 | async-start | bytes 2359296 | tf_op jit(solution)/shard_map/all_gather | solution.py:48
  311.2 172.3 %all-gather.19.cloned.1.call-start = ((), (), s32[]{:S(2)}) async-start(), calls=%async_computation.10 | async-start | bytes 4456448 | tf_op jit(solution)/shard_map/all_gather | solution.py:33
  312.6 211.3 %all-reduce.8.cloned.1.call-start = ((), (), s32[]{:S(2)}) async-start(), calls=%async_computation.6 | async-start | bytes 1048576 | tf_op jit(solution)/shard_map/psum | solution.py:52
  491.7 73.5 %all-gather.15.cloned.1.call-start = ((), (), s32[]{:S(2)}) async-start(), calls=%async_computation.7 | async-start | bytes 2359296 | tf_op jit(solution)/shard_map/all_gather | solution.py:54
  525.6 66.3 %reduce-scatter.2.cloned.1.call-start = ((), (), s32[]{:S(2)}) async-start(), calls=%async_computation.8 | async-start | bytes 786432 | tf_op jit(solution)/shard_map/reduce_scatter | solution.py:60
Sparse Core Ops, SparseCore 0:
  9.5 42.5 all-gather.8
  54.6 130.2 all-gather.16
  193.2 32.0 all-reduce.3
  227.1 39.3 all-gather.10
  274.6 34.7 all-reduce.5
  311.4 39.3 all-gather.12
  353.2 130.2 all-gather.18
  491.8 31.9 all-reduce.7
  525.8 39.3 all-gather.14
  573.3 18.5 reduce-scatter.1
where the time goes:
time: 601 us; the launch traced here: 600 us
  waiting for transfers between devices  542 us (90%)
  matrix products  31.7 us (5%)
  between operations  13.6 us (2%)
  local copies, waits for them, and re-layouts  8.14 us (1%)
    all_gather x2, waiting for transfers between devices, panel_product(): lax.all_gather(left_part, 'col', axis=1, tiled=True)  266 us
    all_gather x2, waiting for transfers between devices, on_device(): lax.all_gather(select_rows(matrix, layer_count, layer_id), 'row', axis=0,...  79.2 us
    all_gather x2, waiting for transfers between devices, on_device(): square_rows = lax.all_gather(own_rows, 'row', axis=0, tiled=True)  79.1 us
    psum x2, waiting for transfers between devices, on_device(): square = lax.psum(partial_value, 'layer')  64.2 us
    psum x1, waiting for transfers between devices, on_device(): matrix = 1.5 * matrix - 0.5 * lax.psum(second, 'layer')  34.9 us
    dot_general x4, matrix products, panel_product(): jnp.dot(lax.all_gather(left_part, 'col', axis=1, tiled=True), right_rows,...  31.7 us
    reduce_scatter x1, waiting for transfers between devices, on_device(): lax.psum_scatter(second, 'layer', scatter_dimension=1, tiled=True)  18.7 us
  transfers between devices with their start and end apart: 10, of which 10 were waited for; matrix products, arithmetic and copies ran while one was open for 0% of the time, Pallas kernels for 0%

commit v1 on v0

v1 whole, which is shorter than its diff:
```python
import jax
import jax.numpy as jnp
from jax import lax
from jax.experimental import pallas as pl
from jax.experimental.pallas import tpu as pltpu
from jax.sharding import PartitionSpec as P

MESH = pl.DeviceIdType.MESH
TILE = 128
ITERS = 2
F32 = jnp.float32
BF16 = jnp.bfloat16
ORDER = (0, 2, 1, 3)


def halves(value):
    high = value.astype(BF16)
    return high, (value - high.astype(F32)).astype(BF16)


def dot3(a_high, a_low, b_high, b_low):
    def dot(a, b):
        return jnp.dot(a, b, preferred_element_type=F32)

    return dot(a_high, b_high) + (dot(a_high, b_low) + dot(a_low, b_high))


def kernel(
    initial, pattern, filters, out,
    own, a_in, b_in, s_in, a_hi, a_lo, b_hi, b_lo, s_hi, s_lo, sq_part, sq_from, pr_part, pr_from,
    a_send, a_recv, y_send, y_recv, g_send, g_recv, e_send, e_recv,
):
    row, col, layer = lax.axis_index("row"), lax.axis_index("col"), lax.axis_index("layer")
    x, y_lo = lax.rem(row, 4), row // 4
    z, y_hi = col // 2, lax.rem(col, 2)
    native = y_hi == layer

    def at_x(step):
        return {"row": y_lo * 4 + lax.rem(x + step + 4, 4)}

    def at_z(step):
        return {"col": lax.rem(z + step + 8, 8) * 2 + y_hi}

    mate_lo = {"row": (1 - y_lo) * 4 + x}
    mate_hi = {"col": z * 2 + (1 - y_hi)}
    sibling = {"layer": 1 - layer}

    barrier = pltpu.get_barrier_semaphore()
    neighbours = (at_x(1), at_x(-1), at_z(1), at_z(-1), mate_lo, mate_hi, sibling)
    for device in neighbours:
        pl.semaphore_signal(barrier, inc=1, device_id=device, device_id_type=MESH)

    def tile_mask(ref, index, value):
        parts = []
        for ct in range(2):
            parts.append(value[:, ct * TILE : (ct + 1) * TILE] * ref[(*index, ct)].astype(F32))
        return jnp.concatenate(parts, axis=1)

    def rows_of(tile):
        return pl.ds(tile * TILE, TILE)

    def remote(src, dst, send, recv, device):
        return pltpu.make_async_remote_copy(
            src_ref=src, dst_ref=dst, send_sem=send, recv_sem=recv, device_id=device, device_id_type=MESH
        )

    def z_copy(it, k, way, depth):
        slot = lax.rem(z - depth + 8, 8) if way == 0 else lax.rem(z + depth, 8)
        piece = a_in.at[it, slot, rows_of(ORDER[k]), :]
        return remote(piece, piece, a_send.at[it, k, way, depth], a_recv.at[it, k, way, depth], at_z(1 if way == 0 else -1))

    def y_copy(it, k):
        piece = a_in.at[it, z, rows_of(ORDER[k]), :]
        return remote(piece, piece, y_send.at[it, k], y_recv.at[it, k], mate_hi)

    def split_a(it, k, slot):
        for part in range(2):
            high, low = halves(a_in[it, slot, rows_of(ORDER[k]), part * TILE : (part + 1) * TILE])
            columns = pl.ds(pl.multiple_of(part * 1024 + slot * TILE, TILE), TILE)
            a_hi[k * TILE : (k + 1) * TILE, columns] = high
            a_lo[k * TILE : (k + 1) * TILE, columns] = low

    def split_b(src, high_ref, low_ref, it, part, slot):
        high, low = halves(src[it, slot, part])
        rows = pl.ds(pl.multiple_of(part * 1024 + slot * TILE, TILE), TILE)
        high_ref[rows, :] = high
        low_ref[rows, :] = low

    class Gather:
        def __init__(self, buf, it, kind, part, finish):
            self.buf, self.it, self.part, self.finish = buf, it, part, finish
            self.base = (it, kind, part)
            self.sent = []

        def copy(self, index, slot, device, half=None):
            piece = self.buf.at[self.it, slot, self.part]
            if half is not None:
                piece = self.buf.at[self.it, slot, self.part, pl.ds(half * 64, 64), :]
            return remote(piece, piece, g_send.at[(*self.base, index)], g_recv.at[(*self.base, index)], device)

        def start(self, copy):
            copy.start()
            self.sent.append(copy)
            return copy

        def slot(self, group, step):
            lane = y_lo if group == 0 else 1 - y_lo
            return lane * 4 + lax.rem(x + step + 4, 4)

        def begin(self):
            self.mate = self.start(self.copy(0, self.slot(0, 0), mate_lo))
            self.spread(0)

        def spread(self, group):
            first = 1 + group * 4
            right = self.start(self.copy(first, self.slot(group, 0), at_x(1)))
            left = self.start(self.copy(first + 1, self.slot(group, 0), at_x(-1)))
            if group == 0:
                self.near = [(right, left)]
            else:
                self.near.append((right, left))

        def from_mate(self):
            self.mate.wait_recv()
            self.spread(1)
            self.finish(self.slot(1, 0))

        def from_near(self, group):
            right, left = self.near[group]
            first = 1 + group * 4
            right.wait_recv()
            far_right = self.start(self.copy(first + 2, self.slot(group, -1), at_x(1), 0))
            self.finish(self.slot(group, -1))
            left.wait_recv()
            far_left = self.start(self.copy(first + 3, self.slot(group, 1), at_x(-1), 1))
            self.finish(self.slot(group, 1))
            if group == 0:
                self.far = [(far_right, far_left)]
            else:
                self.far.append((far_right, far_left))

        def from_far(self, group):
            for copy in self.far[group]:
                copy.wait_recv()
            self.finish(self.slot(group, 2))

        def drain(self):
            for copy in self.sent:
                copy.wait_send()

    def load_tiles(it, part):
        @pl.when(native)
        def _():
            for tile in (part, 2 + part):
                a_in[it, z, rows_of(tile), :] = own[rows_of(tile), :]
                y_copy(it, ORDER.index(tile)).start()

        mine = pl.ds(pl.multiple_of((2 * layer + part) * TILE, TILE), TILE)
        b_in[it, row, part] = own[mine, :]

    for tile in range(4):
        own[rows_of(tile), :] = tile_mask(pattern, (tile,), initial[rows_of(tile), :])
    pl.semaphore_wait(barrier, len(neighbours))

    for it in range(ITERS):
        z_sent = []

        def z_start(k, way, depth):
            copy = z_copy(it, k, way, depth)
            copy.start()
            z_sent.append(copy)

        def z_begin(k):
            if k < 4:
                @pl.when(jnp.logical_not(native))
                def _():
                    y_copy(it, k).wait_recv()

                z_start(k, 0, 0)
                z_start(k, 1, 0)
                split_a(it, k, z)

        def z_step(k, depth):
            for way in range(2):
                if depth == 4 and way != k % 2:
                    continue
                z_copy(it, k, way, depth - 1).wait_recv()
                if depth < 3 or (depth == 3 and way == k % 2):
                    z_start(k, way, depth)
                slot = lax.rem(z - depth + 8, 8) if way == 0 else lax.rem(z + depth, 8)
                split_a(it, k, slot)

        gathers = []

        def gather(buf, kind, part, high_ref, low_ref):
            g = Gather(buf, it, kind, part, lambda slot: split_b(buf, high_ref, low_ref, it, part, slot))
            gathers.append(g)
            return g

        def square(part):
            rows = slice(part * 256, (part + 1) * 256)
            value = dot3(a_hi[rows, :], a_lo[rows, :], b_hi[...], b_lo[...])
            sq_part[it, part, 0] = value[:TILE]
            sq_part[it, part, 1] = value[TILE:]
            copy = remote(
                sq_part.at[it, part, 1 - layer], sq_from.at[it, part],
                e_send.at[it, part], e_recv.at[it, part], sibling,
            )
            copy.start()
            return copy

        def square_ready(part, copy):
            copy.wait_recv()
            value = sq_part[it, part, layer] + sq_from[it, part]
            s_in[it, row, part] = tile_mask(filters, (it, 2 * layer + part), value)
            g = gather(s_in, 1, part, s_hi, s_lo)
            g.begin()
            split_b(s_in, s_hi, s_lo, it, part, row)
            return g

        b0 = gather(b_in, 0, 0, b_hi, b_lo)
        b1 = gather(b_in, 0, 1, b_hi, b_lo)
        load_tiles(it, 0)
        b0.begin()
        load_tiles(it, 1)
        b1.begin()
        split_b(b_in, b_hi, b_lo, it, 0, row)
        split_b(b_in, b_hi, b_lo, it, 1, row)
        z_begin(0)
        z_begin(1)
        b0.from_mate()
        b1.from_mate()
        z_step(0, 1)
        b0.from_near(0)
        z_step(1, 1)
        b1.from_near(0)
        z_step(0, 2)
        b0.from_near(1)
        z_step(1, 2)
        b1.from_near(1)
        z_step(0, 3)
        b0.from_far(0)
        b1.from_far(0)
        z_step(1, 3)
        z_begin(2)
        z_begin(3)
        b0.from_far(1)
        b1.from_far(1)
        z_step(0, 4)
        z_step(1, 4)
        half = square(0)
        z_step(2, 1)
        s0 = square_ready(0, half)
        z_step(3, 1)
        s0.from_mate()
        z_step(2, 2)
        s0.from_near(0)
        z_step(3, 2)
        s0.from_near(1)
        z_step(2, 3)
        s0.from_far(0)
        z_step(3, 3)
        s0.from_far(1)
        z_step(2, 4)
        z_step(3, 4)
        half = square(1)
        s1 = square_ready(1, half)
        s1.from_mate()
        for part in range(2):
            rows = slice(part * 256, (part + 1) * 256)
            pr_part[it, rows, :] = dot3(
                a_hi[rows, :1024], a_lo[rows, :1024], s_hi[:1024, :], s_lo[:1024, :]
            )
        s1.from_near(0)
        s1.from_near(1)
        s1.from_far(0)
        s1.from_far(1)
        copies = []
        for part in range(2):
            rows = slice(part * 256, (part + 1) * 256)
            pr_part[it, rows, :] += dot3(
                a_hi[rows, 1024:], a_lo[rows, 1024:], s_hi[1024:, :], s_lo[1024:, :]
            )
            copy = remote(
                pr_part.at[it, pl.ds(part * 256, 256), :], pr_from.at[it, pl.ds(part * 256, 256), :],
                e_send.at[it, 2 + part], e_recv.at[it, 2 + part], sibling,
            )
            copy.start()
            copies.append(copy)
        for part in range(2):
            copies[part].wait_recv()
            for k in (2 * part, 2 * part + 1):
                tile = ORDER[k]
                rows = slice(k * TILE, (k + 1) * TILE)
                value = tile_mask(filters, (it, tile), pr_part[it, rows, :] + pr_from[it, rows, :])
                own[rows_of(tile), :] = 1.5 * own[rows_of(tile), :] - 0.5 * value

        for copy in z_sent:
            copy.wait_send()
        for g in gathers:
            g.drain()
        for index in range(2):
            remote(
                sq_part.at[it, index, 1 - layer], sq_from.at[it, index],
                e_send.at[it, index], e_recv.at[it, index], sibling,
            ).wait_send()
        for copy in copies:
            copy.wait_send()

        @pl.when(native)
        def _():
            for k in range(4):
                y_copy(it, k).wait_send()

    out[...] = own[:, pl.ds(pl.multiple_of(layer * TILE, TILE), TILE)]


def on_device(initial, pattern, filters):
    dma = pltpu.SemaphoreType.DMA
    vmem = pltpu.VMEM
    return pl.pallas_call(
        kernel,
        out_shape=jax.ShapeDtypeStruct((512, TILE), F32),
        in_specs=[
            pl.BlockSpec(memory_space=pltpu.VMEM),
            pl.BlockSpec(memory_space=pltpu.SMEM),
            pl.BlockSpec(memory_space=pltpu.SMEM),
        ],
        out_specs=pl.BlockSpec(memory_space=pltpu.VMEM),
        scratch_shapes=[
            vmem((512, 256), F32),
            vmem((ITERS, 8, 512, 256), F32),
            vmem((ITERS, 8, 2, TILE, 256), F32),
            vmem((ITERS, 8, 2, TILE, 256), F32),
            vmem((512, 2048), BF16),
            vmem((512, 2048), BF16),
            vmem((2048, 256), BF16),
            vmem((2048, 256), BF16),
            vmem((2048, 256), BF16),
            vmem((2048, 256), BF16),
            vmem((ITERS, 2, 2, TILE, 256), F32),
            vmem((ITERS, 2, TILE, 256), F32),
            vmem((ITERS, 512, 256), F32),
            vmem((ITERS, 512, 256), F32),
            dma((ITERS, 4, 2, 4)),
            dma((ITERS, 4, 2, 4)),
            dma((ITERS, 4)),
            dma((ITERS, 4)),
            dma((ITERS, 2, 2, 9)),
            dma((ITERS, 2, 2, 9)),
            dma((ITERS, 4)),
            dma((ITERS, 4)),
        ],
        compiler_params=pltpu.CompilerParams(
            collective_id=0, has_side_effects=True, vmem_limit_bytes=52 << 20
        ),
        name="sign_iterations",
    )(initial, pattern, filters)


def solution(mesh):
    return jax.shard_map(
        on_device,
        mesh=mesh,
        in_specs=(P("row", "col"), P("row", "col"), P(None, "row", "col")),
        out_specs=P("row", ("col", "layer")),
        check_vma=False,
    )
```

time: 601 us -> 159 us (0.26)
  waiting for transfers between devices: 542 us -> 0 us
  Pallas kernels: 0 us -> 156 us
  matrix products: 31.7 us -> 0 us
  between operations: 13.6 us -> 0.01 us
    all_gather x6 -> x0, waiting for transfers between devices: 424 us -> none  [the longest x2 266 us: panel_product(): lax.all_gather(left_part, 'col', axis=1, tiled=True)]
    pallas_call x0 -> x1, Pallas kernels: none -> 156 us  [on_device(): pl.pallas_call(kernel, out_shape=jax.ShapeDtypeStruct((512, TILE), F32),...]
    psum x3 -> x0, waiting for transfers between devices: 99.1 us -> none  [the longest x2 64.2 us: on_device(): square = lax.psum(partial_value, 'layer')]
    dot_general x4 -> x0, matrix products: 31.7 us -> none  [panel_product(): jnp.dot(lax.all_gather(left_part, 'col', axis=1, tiled=True), right_rows,...]
    reduce_scatter x1 -> x0, waiting for transfers between devices: 18.7 us -> none  [on_device(): lax.psum_scatter(second, 'layer', scatter_dimension=1, tiled=True)]
    dynamic_slice x6 -> x0, local copies, waits for them, and re-layouts: 6.7 us -> none  [the longest x4 4.79 us: select_rows(): chosen = lax.dynamic_index_in_dim(grouped, layer_id, 1, keepdims=False)]
  transfers between devices with their start and end apart: 10 -> 0, of which waited for: 10 -> 0; matrix products, arithmetic and copies ran while one was open for 0% -> 0% of each run, Pallas kernels for 0% -> 0%
where the time goes in v1:
time: 159 us
  Pallas kernels  156 us (98%)
  local copies, waits for them, and re-layouts  2.63 us (2%)
    pallas_call x1, Pallas kernels, on_device(): pl.pallas_call(kernel, out_shape=jax.ShapeDtypeStruct((512, TILE), F32),...  156 us

profile of v1, /device:TPU:1, one launch (start us, length us, event | category | flops | bytes accessed | tf_op | source)
XLA Modules:
  0.0 158.7 jit_solution(15478113725494176005)
XLA Ops:
  0.0 0.0 copy-start.1
  0.0 0.8 copy.4.pattern
  0.8 0.0 copy-done.1
  0.8 0.1 copy.5.filters
  0.9 0.0 copy-start
  0.9 1.0 copy-done
  1.9 156.1 %sign_iterations.1 = f32[512,128]{1,0:T(8,128)S(1)} custom-call(f32[512,256]{1,0:T(8,128)S(1)} %copy-done, s32[4,2]{1,0:T(4,128)S(1)} %copy.4.pattern, s32[2,4,2]{2,1,0:T(4,128)S(1)} %copy.5.filters), custom_call_target="tpu_custom_call" | custom-call | tf_op jit(solution)/shard_map/sign_iterations/pallas_call | solution.py:321
  158.0 0.7 copy.7
Async XLA Ops:
  0.0 0.8 copy-start.1
  0.9 1.0 copy-start

commit v2 on v0

v2 whole, which is shorter than its diff:
```python
import jax
import jax.numpy as jnp
from jax import lax
from jax.experimental import pallas as pl
from jax.experimental.pallas import tpu as pltpu
from jax.sharding import PartitionSpec as P

MESH = pl.DeviceIdType.MESH
TILE = 128
ITERS = 2
PARTS = 4
DEPTH = 64
F32 = jnp.float32
BF16 = jnp.bfloat16
BY_PARTNER = (1, 3)
FAR_BY_MATE = False
STRAIGHT = (3,)
STEPS = [
    ("bg", 0), ("zb", 2), ("y", 1), ("zb", 3), ("zb", 0), ("y", 0), ("gn", "B", 0, 0), ("bg", 1), ("zb", 1),
    ("gm", "B", 0), ("y", 2), ("bg", 3), ("yb", 0), ("gm", "B", 1), ("z", 0, 0, 1), ("bg", 2), ("gf", "B", 0, 0),
    ("yb", 1), ("z", 0, 1, 1), ("gm", "B", 3), ("z", 1, 0, 1), ("gn", "B", 1, 0), ("z", 0, 0, 2),
    ("gn", "B", 3, 0), ("gm", "B", 2), ("z", 0, 1, 2), ("gn", "B", 0, 1), ("y", 3), ("z", 1, 0, 2), ("z", 0, 2, 1),
    ("gn", "B", 2, 0), ("gn", "B", 3, 1), ("z", 1, 1, 1), ("gn", "B", 1, 1), ("yb", 2), ("z", 0, 1, 3),
    ("z", 0, 0, 3), ("gn", "B", 2, 1), ("gf", "B", 1, 0), ("gf", "B", 3, 0), ("z", 1, 0, 3), ("z", 1, 1, 2),
    ("z", 0, 3, 1), ("gf", "B", 2, 0), ("yb", 3), ("gf", "B", 3, 1), ("gf", "B", 1, 1), ("z", 1, 2, 1),
    ("z", 0, 1, 4), ("z", 0, 0, 4), ("gf", "B", 2, 1), ("gf", "B", 0, 1), ("z", 0, 2, 2), ("z", 1, 0, 4),
    ("sq", 0), ("z", 0, 3, 2), ("z", 1, 1, 3), ("z", 1, 2, 2), ("sr", 0), ("z", 1, 1, 4), ("sq", 1),
    ("z", 0, 2, 3), ("sr", 1), ("z", 1, 2, 3), ("z", 1, 3, 1), ("z", 1, 3, 2), ("z", 0, 3, 3), ("gm", "S", 0),
    ("z", 0, 2, 4), ("gm", "S", 1), ("z", 1, 2, 4), ("sq", 2), ("z", 0, 3, 4), ("gn", "S", 0, 0),
    ("gn", "S", 0, 1), ("sr", 2), ("z", 1, 3, 3), ("gn", "S", 1, 0), ("gn", "S", 1, 1), ("z", 1, 3, 4), ("sq", 3),
    ("gm", "S", 2), ("gf", "S", 0, 0), ("sr", 3), ("gf", "S", 1, 1), ("gn", "S", 2, 1), ("gf", "S", 0, 1),
    ("gf", "S", 1, 0), ("gn", "S", 2, 0), ("pr0", 1), ("gd", "S", 3, 0), ("pr0", 0), ("gf", "S", 2, 0),
    ("gf", "S", 2, 1), ("gd", "S", 3, 1),
]


def halves(value):
    high = value.astype(BF16)
    return high, (value - high.astype(F32)).astype(BF16)


def dot3(a_high, a_low, b_high, b_low):
    def dot(a, b):
        return jnp.dot(a, b, preferred_element_type=F32)

    return dot(a_high, b_high) + (dot(a_high, b_low) + dot(a_low, b_high))


def kernel(
    initial, pattern, filters, out,
    own, a_in, b_in, s_in, a_hi, a_lo, b_hi, b_lo, s_hi, s_lo, sq_part, sq_from, pr_part, pr_from,
    a_send, a_recv, y_send, y_recv, p_send, p_recv, g_send, g_recv, e_send, e_recv,
):
    row, col, layer = lax.axis_index("row"), lax.axis_index("col"), lax.axis_index("layer")
    x, y_lo = lax.rem(row, 4), row // 4
    z, y_hi = col // 2, lax.rem(col, 2)
    def at_x(step):
        return {"row": y_lo * 4 + lax.rem(x + step + 4, 4)}

    def at_z(step):
        return {"col": lax.rem(z + step + 8, 8) * 2 + y_hi}

    def mate_x(step):
        return {"row": (1 - y_lo) * 4 + lax.rem(x + step + 4, 4)}

    mate_lo = mate_x(0)
    mate_hi = {"col": z * 2 + (1 - y_hi)}
    sibling = {"layer": 1 - layer}

    barrier = pltpu.get_barrier_semaphore()
    neighbours = (at_x(1), at_x(-1), at_z(1), at_z(-1), mate_lo, mate_hi, sibling)
    if STRAIGHT:
        neighbours += (at_x(2), mate_x(1), mate_x(-1), mate_x(2))
    for device in neighbours:
        pl.semaphore_signal(barrier, inc=1, device_id=device, device_id_type=MESH)

    def tile_mask(ref, index, value):
        parts = []
        for ct in range(2):
            parts.append(value[:, ct * TILE : (ct + 1) * TILE] * ref[(*index, ct)].astype(F32))
        return jnp.concatenate(parts, axis=1)

    def remote(src, dst, send, recv, device):
        return pltpu.make_async_remote_copy(
            src_ref=src, dst_ref=dst, send_sem=send, recv_sem=recv, device_id=device, device_id_type=MESH
        )

    def z_slot(group, way, depth):
        at = lax.rem(z - depth + 8, 8) if way == 0 else lax.rem(z + depth, 8)
        return 2 * at + (y_hi if group == 0 else 1 - y_hi)

    def far_way(group, k):
        return k % 2 if k in BY_PARTNER else (k + group) % 2

    def a_piece(it, k, slot):
        return a_in.at[it, slot, k // 2, :, k % 2]

    def z_copy(it, group, k, way, depth):
        piece = a_piece(it, k, z_slot(group, way, depth))
        place = (it, group, k, way, depth)
        return remote(piece, piece, a_send.at[place], a_recv.at[place], at_z(1 - 2 * way))

    def y_copy(it, k):
        piece = a_piece(it, k, col)
        return remote(piece, piece, y_send.at[it, k], y_recv.at[it, k], mate_hi)

    def p_copy(it, k, way, depth):
        piece = a_piece(it, k, z_slot(0, way, depth))
        place = (it, BY_PARTNER.index(k), way, depth - 1)
        return remote(piece, piece, p_send.at[place], p_recv.at[place], mate_hi)

    def split_a(it, k, slot):
        columns = pl.ds(pl.multiple_of(lax.rem(slot, 2) * 1024 + slot // 2 * TILE, TILE), TILE)
        for side in range(2):
            rows = slice((2 * k + side) * DEPTH, (2 * k + side + 1) * DEPTH)
            high, low = halves(a_in[it, slot, k // 2, side, k % 2])
            a_hi[rows, columns] = high
            a_lo[rows, columns] = low

    bufs = {"B": (b_in, b_hi, b_lo), "S": (s_in, s_hi, s_lo)}

    def split_b(it, kind, part, slot):
        buf, high_ref, low_ref = bufs[kind]
        high, low = halves(buf[it, slot, part])
        rows = pl.ds(pl.multiple_of(part // 2 * 1024 + slot * TILE + part % 2 * DEPTH, DEPTH), DEPTH)
        high_ref[rows, :] = high
        low_ref[rows, :] = low

    def g_slot(group, step):
        lane = y_lo if group == 0 else 1 - y_lo
        return lane * 4 + lax.rem(x + step + 4, 4)

    def g_copy(it, kind, part, what):
        way = (part + what - 5) % 2
        if kind == "S" and part in STRAIGHT:
            slot = row
            device = (mate_lo, at_x(1), at_x(-1), mate_x(1), mate_x(-1), at_x(2), mate_x(2))[what]
        elif what == 0:
            slot, device = g_slot(0, 0), mate_lo
        elif what < 5:
            slot, device = g_slot((what - 1) // 2, 0), at_x(1 if what % 2 else -1)
        elif what == 6 and FAR_BY_MATE:
            slot, device = g_slot(0, 2), mate_lo
        else:
            slot, device = g_slot(what - 5, 2 * way - 1), at_x(1 - 2 * way)
        piece = bufs[kind][0].at[it, slot, part]
        place = (it, "BS".index(kind), part, what)
        return remote(piece, piece, g_send.at[place], g_recv.at[place], device)

    def e_copy(it, part):
        return remote(
            sq_part.at[it, part, 1 - layer], sq_from.at[it, part], e_send.at[it, part], e_recv.at[it, part], sibling
        )

    def pr_copy(it, part):
        rows = pl.ds(part * 256, 256)
        columns = slice(None)
        if it == ITERS - 1:
            columns = pl.ds(pl.multiple_of((1 - layer) * TILE, TILE), TILE)
        return remote(
            pr_part.at[it, rows, columns], pr_from.at[it, rows, columns],
            e_send.at[it, PARTS + part], e_recv.at[it, PARTS + part], sibling,
        )

    mine = pl.ds(pl.multiple_of(layer * TILE, TILE), TILE)

    def own_part(it, part):
        a_in[it, col, part // 2, :, part % 2] = own[part // 2, :, part % 2, :, mine]
        split_a(it, part, col)
        b_in[it, row, part] = own[part // 2, layer, part % 2]
        split_b(it, "B", part, row)

    def iteration(it):
        def y_begin(k):
            y_copy(it, k).start()

        def z_begin(k):
            z_copy(it, 0, k, 0, 0).start()
            z_copy(it, 0, k, 1, 0).start()

        def y_arrives(k):
            y_copy(it, k).wait_recv()
            if k not in BY_PARTNER:
                z_copy(it, 1, k, 0, 0).start()
                z_copy(it, 1, k, 1, 0).start()
            split_a(it, k, z_slot(1, 0, 0))

        def z_arrives(group, k, depth):
            for way in range(2):
                if depth == 4 and way != far_way(group, k):
                    continue
                if group == 1 and k in BY_PARTNER:
                    p_copy(it, k, way, depth).wait_recv()
                else:
                    z_copy(it, group, k, way, depth - 1).wait_recv()
                    if depth < 3 or (depth == 3 and way == far_way(group, k)):
                        z_copy(it, group, k, way, depth).start()
                    if k in BY_PARTNER:
                        p_copy(it, k, way, depth).start()
                split_a(it, k, z_slot(group, way, depth))

        def column_begin(part):
            for what in range(3):
                g_copy(it, "B", part, what).start()

        def straight(kind, part, far):
            for what in (3, 4, 5, 6) if far else (0, 1, 2):
                g_copy(it, kind, part, what).wait_recv()
                slot = (
                    g_slot(1, 0), g_slot(0, -1), g_slot(0, 1), g_slot(1, -1), g_slot(1, 1), g_slot(0, 2), g_slot(1, 2)
                )[what]
                split_b(it, kind, part, slot)

        def from_mate(kind, part):
            g_copy(it, kind, part, 0).wait_recv()
            g_copy(it, kind, part, 3).start()
            g_copy(it, kind, part, 4).start()
            split_b(it, kind, part, g_slot(1, 0))

        def from_near(kind, part, group):
            for way in range(2):
                g_copy(it, kind, part, 1 + 2 * group + way).wait_recv()
                if way == (part + group) % 2 and not (group == 1 and FAR_BY_MATE):
                    g_copy(it, kind, part, 5 + group).start()
                split_b(it, kind, part, g_slot(group, 2 * way - 1))

        def from_far(kind, part, group):
            g_copy(it, kind, part, 5 + group).wait_recv()
            if group == 0 and FAR_BY_MATE:
                g_copy(it, kind, part, 6).start()
            split_b(it, kind, part, g_slot(group, 2))

        def square(part):
            rows = slice(part * TILE, (part + 1) * TILE)
            value = dot3(a_hi[rows, :], a_lo[rows, :], b_hi[...], b_lo[...])
            sq_part[it, part, 0] = value[:DEPTH]
            sq_part[it, part, 1] = value[DEPTH:]
            e_copy(it, part).start()

        def square_ready(part):
            e_copy(it, part).wait_recv()
            value = sq_part[it, part, layer] + sq_from[it, part]
            s_in[it, row, part] = tile_mask(filters, (it, 2 * (part // 2) + layer), value)
            for what in range(7 if part in STRAIGHT else 3):
                g_copy(it, "S", part, what).start()
            split_b(it, "S", part, row)

        def product(first, part):
            rows = slice(part * 256, (part + 1) * 256)
            depth = slice(0, 1024) if first else slice(1024, 2048)
            value = dot3(a_hi[rows, depth], a_lo[rows, depth], s_hi[depth, :], s_lo[depth, :])
            if first:
                pr_part[it, rows, :] = value
            else:
                pr_part[it, rows, :] += value
                pr_copy(it, part).start()

        def update(part):
            pr_copy(it, part).wait_recv()
            for half in range(2):
                for side in range(2):
                    at = (4 * part + 2 * half + side) * DEPTH
                    rows = slice(at, at + DEPTH)
                    place = (part, side, half)
                    if it < ITERS - 1:
                        value = tile_mask(filters, (it, 2 * part + side), pr_part[it, rows, :] + pr_from[it, rows, :])
                        own[place] = 1.5 * own[place] - 0.5 * value
                    else:
                        value = (pr_part[it, rows, mine] + pr_from[it, rows, mine]) * filters[
                            it, 2 * part + side, layer
                        ].astype(F32)
                        out[place] = 1.5 * own[(*place, slice(None), mine)] - 0.5 * value

        run = {
            "y": y_begin, "zb": z_begin, "yb": y_arrives, "z": z_arrives, "bg": column_begin, "gm": from_mate,
            "gn": from_near, "gf": from_far, "gd": straight, "sq": square, "sr": square_ready,
            "pr0": lambda part: product(True, part),
        }
        for step in STEPS:
            run[step[0]](*step[1:])
        product(False, 0)
        product(False, 1)
        return update

    def drain(it):
        for k in range(PARTS):
            for group in range(2):
                for way in range(2):
                    for depth in range(4):
                        if depth < 3 or way == far_way(group, k):
                            if group == 0 or k not in BY_PARTNER:
                                z_copy(it, group, k, way, depth).wait_send()
                            if group == 0 and k in BY_PARTNER:
                                p_copy(it, k, way, depth + 1).wait_send()
            for kind in "BS":
                for what in range(7):
                    g_copy(it, kind, k, what).wait_send()
            y_copy(it, k).wait_send()
            e_copy(it, k).wait_send()
        pr_copy(it, 0).wait_send()
        pr_copy(it, 1).wait_send()

    for tile in range(4):
        for half in range(2):
            place = (tile // 2, tile % 2, half)
            own[place] = tile_mask(pattern, (tile,), initial[place])
    pl.semaphore_wait(barrier, len(neighbours))
    for part in range(PARTS):
        own_part(0, part)
    for it in range(ITERS):
        update = iteration(it)
        for part in range(2):
            update(part)
            if it + 1 < ITERS:
                own_part(it + 1, 2 * part)
                own_part(it + 1, 2 * part + 1)
    for it in range(ITERS):
        drain(it)


def on_device(initial, pattern, filters):
    dma = pltpu.SemaphoreType.DMA
    vmem = pltpu.VMEM
    out = pl.pallas_call(
        kernel,
        out_shape=jax.ShapeDtypeStruct((2, 2, 2, DEPTH, TILE), F32),
        in_specs=[
            pl.BlockSpec(memory_space=pltpu.VMEM),
            pl.BlockSpec(memory_space=pltpu.SMEM),
            pl.BlockSpec(memory_space=pltpu.SMEM),
        ],
        out_specs=pl.BlockSpec(memory_space=pltpu.VMEM),
        scratch_shapes=[
            vmem((2, 2, 2, DEPTH, 256), F32),
            vmem((ITERS, 16, 2, 2, 2, DEPTH, TILE), F32),
            vmem((ITERS, 8, PARTS, DEPTH, 256), F32),
            vmem((ITERS, 8, PARTS, DEPTH, 256), F32),
            vmem((512, 2048), BF16),
            vmem((512, 2048), BF16),
            vmem((2048, 256), BF16),
            vmem((2048, 256), BF16),
            vmem((2048, 256), BF16),
            vmem((2048, 256), BF16),
            vmem((ITERS, PARTS, 2, DEPTH, 256), F32),
            vmem((ITERS, PARTS, DEPTH, 256), F32),
            vmem((ITERS, 512, 256), F32),
            vmem((ITERS, 512, 256), F32),
            dma((ITERS, 2, PARTS, 2, 4)),
            dma((ITERS, 2, PARTS, 2, 4)),
            dma((ITERS, PARTS)),
            dma((ITERS, PARTS)),
            dma((ITERS, max(1, len(BY_PARTNER)), 2, 4)),
            dma((ITERS, max(1, len(BY_PARTNER)), 2, 4)),
            dma((ITERS, 2, PARTS, 7)),
            dma((ITERS, 2, PARTS, 7)),
            dma((ITERS, PARTS + 2)),
            dma((ITERS, PARTS + 2)),
        ],
        compiler_params=pltpu.CompilerParams(
            collective_id=0, has_side_effects=True, vmem_limit_bytes=52 << 20
        ),
        name="sign_iterations",
    )(initial.reshape(2, 2, 2, DEPTH, 256), pattern, filters)
    return out.reshape(512, TILE)


def solution(mesh):
    return jax.shard_map(
        on_device,
        mesh=mesh,
        in_specs=(P("row", "col"), P("row", "col"), P(None, "row", "col")),
        out_specs=P("row", ("col", "layer")),
        check_vma=False,
    )
```

time: 601 us -> 130 us (0.22)
  waiting for transfers between devices: 542 us -> 0 us
  Pallas kernels: 0 us -> 128 us
  matrix products: 31.7 us -> 0 us
  between operations: 13.6 us -> 0.01 us
    all_gather x6 -> x0, waiting for transfers between devices: 424 us -> none  [the longest x2 266 us: panel_product(): lax.all_gather(left_part, 'col', axis=1, tiled=True)]
    pallas_call x0 -> x1, Pallas kernels: none -> 128 us  [on_device(): pl.pallas_call(kernel, out_shape=jax.ShapeDtypeStruct((2, 2, 2, DEPTH, TI...]
    psum x3 -> x0, waiting for transfers between devices: 99.1 us -> none  [the longest x2 64.2 us: on_device(): square = lax.psum(partial_value, 'layer')]
    dot_general x4 -> x0, matrix products: 31.7 us -> none  [panel_product(): jnp.dot(lax.all_gather(left_part, 'col', axis=1, tiled=True), right_rows,...]
    reduce_scatter x1 -> x0, waiting for transfers between devices: 18.7 us -> none  [on_device(): lax.psum_scatter(second, 'layer', scatter_dimension=1, tiled=True)]
    dynamic_slice x6 -> x0, local copies, waits for them, and re-layouts: 6.7 us -> none  [the longest x4 4.79 us: select_rows(): chosen = lax.dynamic_index_in_dim(grouped, layer_id, 1, keepdims=False)]
  transfers between devices with their start and end apart: 10 -> 0, of which waited for: 10 -> 0; matrix products, arithmetic and copies ran while one was open for 0% -> 0% of each run, Pallas kernels for 0% -> 0%
where the time goes in v2:
time: 130 us
  Pallas kernels  128 us (98%)
  local copies, waits for them, and re-layouts  2.63 us (2%)
    pallas_call x1, Pallas kernels, on_device(): pl.pallas_call(kernel, out_shape=jax.ShapeDtypeStruct((2, 2, 2, DEPTH, TI...  128 us
    unnamed x7, local copies, waits for them, and re-layouts  2.63 us

profile of v2, /device:TPU:1, one launch (start us, length us, event | category | flops | bytes accessed | tf_op | source)
XLA Modules:
  0.0 130.2 jit_solution(9596673242798663811)
XLA Ops:
  0.0 0.0 copy-start.1
  0.0 0.8 copy.4.pattern
  0.8 0.0 copy-done.1
  0.8 0.1 copy.5.filters
  0.9 0.0 copy-start
  0.9 1.0 copy-done
  1.9 127.5 %sign_iterations.1 = f32[2,2,2,64,128]{4,3,2,1,0:T(8,128)S(1)} custom-call(f32[2,2,2,64,256]{4,3,2,1,0:T(8,128)S(1)} %bitcast.3, s32[4,2]{1,0:T(4,128)S(1)} %copy.4.pattern, s32[2,4,2]{2,1,0:T(4,128)S(1)} %copy.5.filters), custom_call_target="tpu_custom_call" | custom-call | tf_op jit(solution)/shard_map/sign_iterations/pallas_call | solution.py:324
  129.5 0.7 copy.7
Async XLA Ops:
  0.0 0.8 copy-start.1
  0.9 1.0 copy-start

commit v3 on v2

v3 whole, which is shorter than its diff:
```python
import jax
import jax.numpy as jnp
from jax import lax
from jax.experimental import pallas as pl
from jax.experimental.pallas import tpu as pltpu
from jax.sharding import PartitionSpec as P

MESH = pl.DeviceIdType.MESH
TILE = 128
ITERS = 2
SIZES = (64, 64, 64, 32, 32)
PARTS = len(SIZES)
STARTS = tuple(sum(SIZES[:k]) for k in range(PARTS))
F32 = jnp.float32
BF16 = jnp.bfloat16
BY_PARTNER = (1,)
FAR_BY_MATE = "S"
STRAIGHT = (4,)
STEPS = [
    ("ox", 0), ("zb", 1), ("y", 0), ("ox", 1), ("zb", 3), ("bg", 4), ("y", 3), ("zb", 2), ("y", 4), ("zb", 0),
    ("bg", 2), ("bg", 3), ("bg", 0), ("yb", 0), ("gm", "B", 4), ("y", 1), ("y", 2), ("bg", 1), ("gn", "B", 4, 0),
    ("z", 0, 3, 1), ("z", 0, 1, 1), ("gn", "B", 2, 0), ("z", 0, 0, 1), ("gm", "B", 2), ("gm", "B", 3), ("yb", 3),
    ("yb", 4), ("z", 1, 0, 1), ("z", 0, 1, 2), ("gn", "B", 1, 0), ("gm", "B", 0), ("yb", 2), ("gn", "B", 0, 0),
    ("z", 1, 3, 1), ("gf", "B", 4, 0), ("z", 0, 0, 2), ("gn", "B", 3, 0), ("gm", "B", 1), ("z", 0, 1, 3),
    ("gn", "B", 0, 1), ("yb", 1), ("gn", "B", 3, 1), ("gn", "B", 4, 1), ("z", 1, 0, 2), ("z", 1, 2, 1),
    ("gn", "B", 1, 1), ("z", 1, 3, 2), ("z", 0, 3, 2), ("gn", "B", 2, 1), ("z", 0, 2, 1), ("z", 0, 1, 4),
    ("gf", "B", 4, 1), ("gf", "B", 2, 0), ("z", 0, 0, 3), ("z", 1, 1, 1), ("z", 1, 0, 3), ("gf", "B", 3, 1),
    ("gf", "B", 1, 0), ("z", 1, 1, 2), ("gf", "B", 0, 0), ("gf", "B", 1, 1), ("gf", "B", 3, 0), ("gf", "B", 2, 1),
    ("z", 1, 1, 3), ("z", 1, 2, 2), ("z", 1, 3, 3), ("z", 1, 1, 4), ("zb", 4), ("gf", "B", 0, 1), ("sq", 1),
    ("z", 0, 3, 3), ("z", 1, 4, 1), ("z", 0, 0, 4), ("z", 0, 2, 2), ("sr", 1), ("z", 1, 0, 4), ("sq", 0),
    ("z", 0, 4, 1), ("z", 1, 3, 4), ("z", 1, 2, 3), ("sr", 0), ("z", 1, 4, 2), ("z", 0, 2, 3), ("gm", "S", 1),
    ("z", 0, 3, 4), ("sq", 3), ("gn", "S", 1, 0), ("z", 0, 4, 2), ("gn", "S", 0, 0), ("gm", "S", 0), ("sr", 3),
    ("z", 0, 2, 4), ("z", 1, 2, 4), ("sq", 2), ("z", 1, 4, 3), ("z", 0, 4, 3), ("sr", 2), ("gf", "S", 0, 0),
    ("gf", "S", 1, 0), ("z", 0, 4, 4), ("gm", "S", 3), ("z", 1, 4, 4), ("sq", 4), ("gn", "S", 3, 0),
    ("gn", "S", 2, 0), ("sr", 4), ("gn", "S", 1, 1), ("gn", "S", 0, 1), ("gf", "S", 3, 0), ("gn", "S", 3, 1),
    ("gf", "S", 2, 0), ("gm", "S", 2), ("gd", "S", 4, 0), ("gf", "S", 1, 1), ("gf", "S", 0, 1), ("pr0", 0),
    ("pr0", 1), ("gf", "S", 3, 1), ("gd", "S", 4, 1), ("gn", "S", 2, 1), ("gf", "S", 2, 1),
]


def halves(value):
    high = value.astype(BF16)
    return high, (value - high.astype(F32)).astype(BF16)


def dot3(a_high, a_low, b_high, b_low):
    def dot(a, b):
        return jnp.dot(a, b, preferred_element_type=F32)

    return dot(a_high, b_high) + (dot(a_high, b_low) + dot(a_low, b_high))


def kernel(
    initial, pattern_in, filters_in, out,
    raw, pattern, filters, own, a_in, b_in, s_in, a_hi, a_lo, b_hi, b_lo, s_hi, s_lo, sq_part, sq_from, pr_part, pr_from,
    sent, a_recv, y_recv, p_recv, g_recv, e_recv, in_sem,
):
    row, col, layer = lax.axis_index("row"), lax.axis_index("col"), lax.axis_index("layer")
    x, y_lo = lax.rem(row, 4), row // 4
    z, y_hi = col // 2, lax.rem(col, 2)
    def at_x(step):
        return {"row": y_lo * 4 + lax.rem(x + step + 4, 4)}

    def at_z(step):
        return {"col": lax.rem(z + step + 8, 8) * 2 + y_hi}

    def mate_x(step):
        return {"row": (1 - y_lo) * 4 + lax.rem(x + step + 4, 4)}

    mate_lo = mate_x(0)
    mate_hi = {"col": z * 2 + (1 - y_hi)}
    sibling = {"layer": 1 - layer}

    barrier = pltpu.get_barrier_semaphore()
    neighbours = (at_x(1), at_x(-1), at_z(1), at_z(-1), mate_lo, mate_hi, sibling)
    if STRAIGHT:
        neighbours += (at_x(2), mate_x(1), mate_x(-1), mate_x(2))
    for device in neighbours:
        pl.semaphore_signal(barrier, inc=1, device_id=device, device_id_type=MESH)

    def half_of(k):
        return STARTS[k] // TILE

    def span(k):
        return pl.ds(STARTS[k] % TILE, SIZES[k])

    def tile_mask(ref, index, value):
        parts = []
        for ct in range(2):
            parts.append(value[:, ct * TILE : (ct + 1) * TILE] * ref[(*index, ct)].astype(F32))
        return jnp.concatenate(parts, axis=1)

    def remote(src, dst, send, recv, device):
        return pltpu.make_async_remote_copy(
            src_ref=src, dst_ref=dst, send_sem=send, recv_sem=recv, device_id=device, device_id_type=MESH
        )

    def z_slot(group, way, depth):
        at = lax.rem(z - depth + 8, 8) if way == 0 else lax.rem(z + depth, 8)
        return 2 * at + (y_hi if group == 0 else 1 - y_hi)

    def far_way(group, k):
        return k % 2 if k in BY_PARTNER else (k + group) % 2

    def a_piece(it, k, slot):
        return a_in.at[it, slot, pl.ds(2 * STARTS[k], 2 * SIZES[k])]

    def z_copy(it, group, k, way, depth):
        piece = a_piece(it, k, z_slot(group, way, depth))
        return remote(piece, piece, sent.at[0], a_recv.at[it, group, k, depth], at_z(1 - 2 * way))

    def a_wait(it, k, depth, recv):
        pieces = a_in.at[it, pl.ds(0, 1 if depth == 4 else 2), pl.ds(2 * STARTS[k], 2 * SIZES[k])]
        remote(pieces, pieces, sent.at[0], recv, mate_hi).wait_recv()

    def y_copy(it, k):
        piece = a_piece(it, k, col)
        return remote(piece, piece, sent.at[0], y_recv.at[it, k], mate_hi)

    def p_copy(it, k, way, depth):
        piece = a_piece(it, k, z_slot(0, way, depth))
        return remote(piece, piece, sent.at[0], p_recv.at[it, BY_PARTNER.index(k), depth - 1], mate_hi)

    def split_a(it, k, slot):
        columns = pl.ds(pl.multiple_of(lax.rem(slot, 2) * 1024 + slot // 2 * TILE, TILE), TILE)
        rows = slice(2 * STARTS[k], 2 * (STARTS[k] + SIZES[k]))
        high, low = halves(a_in[it, slot, rows])
        a_hi[rows, columns] = high
        a_lo[rows, columns] = low

    bufs = {"B": (b_in, b_hi, b_lo), "S": (s_in, s_hi, s_lo)}

    def split_b(it, kind, part, slot):
        buf, high_ref, low_ref = bufs[kind]
        high, low = halves(buf[it, slot, half_of(part), span(part)])
        rows = pl.ds(pl.multiple_of(half_of(part) * 1024 + slot * TILE + STARTS[part] % TILE, 16), SIZES[part])
        high_ref[rows, :] = high
        low_ref[rows, :] = low

    def g_slot(group, step):
        lane = y_lo if group == 0 else 1 - y_lo
        return lane * 4 + lax.rem(x + step + 4, 4)

    def g_copy(it, kind, part, what):
        way = (part + what - 5) % 2
        if kind == "S" and part in STRAIGHT:
            slot = row
            device = (mate_lo, at_x(1), at_x(-1), mate_x(1), mate_x(-1), at_x(2), mate_x(2))[what]
        elif what == 0:
            slot, device = g_slot(0, 0), mate_lo
        elif what < 5:
            slot, device = g_slot((what - 1) // 2, 0), at_x(1 if what % 2 else -1)
        elif what == 6 and kind in FAR_BY_MATE:
            slot, device = g_slot(0, 2), mate_lo
        else:
            slot, device = g_slot(what - 5, 2 * way - 1), at_x(1 - 2 * way)
        piece = bufs[kind][0].at[it, slot, half_of(part), span(part)]
        return remote(piece, piece, sent.at[1 + "BS".index(kind)], g_sem(it, kind, part, what), device)

    def g_sem(it, kind, part, what):
        straight_on = kind == "S" and part in STRAIGHT
        return g_recv.at[it, "BS".index(kind), part, int(what > 2) if straight_on else (0, 1, 1, 2, 2, 3, 4)[what]]

    def g_wait(it, kind, part, what, count):
        pieces = bufs[kind][0].at[it, pl.ds(0, count), half_of(part), span(part)]
        remote(pieces, pieces, sent.at[1 + "BS".index(kind)], g_sem(it, kind, part, what), mate_lo).wait_recv()

    def rows_of(part):
        return pl.ds(STARTS[part], SIZES[part])

    def e_copy(it, part):
        return remote(
            sq_part.at[it, 1 - layer, rows_of(part)], sq_from.at[it, rows_of(part)], sent.at[3], e_recv.at[it, part], sibling
        )

    def pr_copy(it, part):
        rows = pl.ds(part * 256, 256)
        columns = slice(None)
        if it == ITERS - 1:
            columns = pl.ds(pl.multiple_of((1 - layer) * TILE, TILE), TILE)
        return remote(
            pr_part.at[it, rows, columns], pr_from.at[it, rows, columns],
            sent.at[4 + it], e_recv.at[it, PARTS + part], sibling,
        )

    mine = pl.ds(pl.multiple_of(layer * TILE, TILE), TILE)

    def own_part(it, part):
        for side in range(2):
            rows = pl.ds(2 * STARTS[part] + side * SIZES[part], SIZES[part])
            a_in[it, col, rows] = own[half_of(part), side, span(part), mine]
        split_a(it, part, col)
        b_in[it, row, half_of(part), span(part)] = own[half_of(part), layer, span(part)]
        split_b(it, "B", part, row)

    def iteration(it, update_before):
        def y_begin(k):
            y_copy(it, k).start()

        def z_begin(k):
            z_copy(it, 0, k, 0, 0).start()
            z_copy(it, 0, k, 1, 0).start()

        def y_arrives(k):
            y_copy(it, k).wait_recv()
            if k not in BY_PARTNER:
                z_copy(it, 1, k, 0, 0).start()
                z_copy(it, 1, k, 1, 0).start()
            split_a(it, k, z_slot(1, 0, 0))

        def z_arrives(group, k, depth):
            ways = [way for way in range(2) if depth < 4 or way == far_way(group, k)]
            if group == 1 and k in BY_PARTNER:
                a_wait(it, k, depth, p_recv.at[it, BY_PARTNER.index(k), depth - 1])
            else:
                a_wait(it, k, depth, a_recv.at[it, group, k, depth - 1])
                for way in ways:
                    if depth < 3 or (depth == 3 and way == far_way(group, k)):
                        z_copy(it, group, k, way, depth).start()
                    if k in BY_PARTNER:
                        p_copy(it, k, way, depth).start()
            for way in ways:
                split_a(it, k, z_slot(group, way, depth))

        def column_begin(part):
            for what in range(3):
                g_copy(it, "B", part, what).start()

        def straight(kind, part, far):
            whats = (3, 4, 5, 6) if far else (0, 1, 2)
            g_wait(it, kind, part, whats[0], len(whats))
            slots = (g_slot(1, 0), g_slot(0, -1), g_slot(0, 1), g_slot(1, -1), g_slot(1, 1), g_slot(0, 2), g_slot(1, 2))
            for what in whats:
                split_b(it, kind, part, slots[what])

        def from_mate(kind, part):
            g_wait(it, kind, part, 0, 1)
            g_copy(it, kind, part, 3).start()
            g_copy(it, kind, part, 4).start()
            split_b(it, kind, part, g_slot(1, 0))

        def from_near(kind, part, group):
            g_wait(it, kind, part, 1 + 2 * group, 2)
            for way in range(2):
                if way == (part + group) % 2 and not (group == 1 and kind in FAR_BY_MATE):
                    g_copy(it, kind, part, 5 + group).start()
                split_b(it, kind, part, g_slot(group, 2 * way - 1))

        def from_far(kind, part, group):
            g_wait(it, kind, part, 5 + group, 1)
            if group == 0 and kind in FAR_BY_MATE:
                g_copy(it, kind, part, 6).start()
            split_b(it, kind, part, g_slot(group, 2))

        def square(part):
            rows = slice(2 * STARTS[part], 2 * (STARTS[part] + SIZES[part]))
            value = dot3(a_hi[rows, :], a_lo[rows, :], b_hi[...], b_lo[...])
            sq_part[it, 0, rows_of(part)] = value[: SIZES[part]]
            sq_part[it, 1, rows_of(part)] = value[SIZES[part] :]
            e_copy(it, part).start()

        def square_ready(part):
            e_copy(it, part).wait_recv()
            value = sq_part[it, layer, rows_of(part)] + sq_from[it, rows_of(part)]
            s_in[it, row, half_of(part), span(part)] = tile_mask(filters, (it, 2 * half_of(part) + layer), value)
            for what in range(7 if part in STRAIGHT else 3):
                g_copy(it, "S", part, what).start()
            split_b(it, "S", part, row)

        def product(first, part):
            rows = slice(part * 256, (part + 1) * 256)
            depth = slice(0, 1024) if first else slice(1024, 2048)
            value = dot3(a_hi[rows, depth], a_lo[rows, depth], s_hi[depth, :], s_lo[depth, :])
            if first:
                pr_part[it, rows, :] = value
            else:
                pr_part[it, rows, :] += value
                pr_copy(it, part).start()

        def update(part):
            pr_copy(it, part).wait_recv()
            for k in range(PARTS):
                for side in range(2):
                    if half_of(k) != part:
                        continue
                    at = 2 * STARTS[k] + side * SIZES[k]
                    rows = slice(at, at + SIZES[k])
                    place = (part, side, span(k))
                    if it < ITERS - 1:
                        value = tile_mask(filters, (it, 2 * part + side), pr_part[it, rows, :] + pr_from[it, rows, :])
                        own[place] = 1.5 * own[place] - 0.5 * value
                    else:
                        value = (pr_part[it, rows, mine] + pr_from[it, rows, mine]) * filters[
                            it, 2 * part + side, layer
                        ].astype(F32)
                        out[place] = 1.5 * own[(*place, mine)] - 0.5 * value

        def own_half(part):
            if update_before is not None:
                update_before(part)
            else:
                for side in range(2):
                    own[part, side] = tile_mask(pattern, (2 * part + side,), raw[part, side])
            for k in range(PARTS):
                if half_of(k) == part:
                    own_part(it, k)

        run = {
            "ox": own_half,
            "y": y_begin, "zb": z_begin, "yb": y_arrives, "z": z_arrives, "bg": column_begin, "gm": from_mate,
            "gn": from_near, "gf": from_far, "gd": straight, "sq": square, "sr": square_ready,
            "pr0": lambda part: product(True, part),
        }
        for step in STEPS:
            run[step[0]](*step[1:])
        product(False, 0)
        product(False, 1)
        return update

    fetch = [
        pltpu.make_async_copy(src, dst, in_sem.at[index])
        for index, (src, dst) in enumerate(((initial, raw), (pattern_in, pattern), (filters_in, filters)))
    ]
    for copy in fetch:
        copy.start()
    for copy in fetch:
        copy.wait()
    pl.semaphore_wait(barrier, len(neighbours))
    before = None
    for it in range(ITERS):
        before = iteration(it, before)
    before(0)
    before(1)
    pieces = (a_in.at[:, pl.ds(0, 15)], b_in.at[:, pl.ds(0, 7)], s_in.at[:, pl.ds(0, 7)], sq_from, pr_from.at[0], pr_from.at[1, :, mine])
    for index, piece in enumerate(pieces):
        remote(piece, piece, sent.at[index], in_sem.at[0], sibling).wait_send()


def on_device(initial, pattern, filters):
    dma = pltpu.SemaphoreType.DMA
    vmem = pltpu.VMEM
    out = pl.pallas_call(
        kernel,
        out_shape=jax.ShapeDtypeStruct((2, 2, TILE, TILE), F32),
        in_specs=[
            pl.BlockSpec(memory_space=pltpu.HBM),
            pl.BlockSpec(memory_space=pl.ANY),
            pl.BlockSpec(memory_space=pl.ANY),
        ],
        out_specs=pl.BlockSpec(memory_space=pltpu.VMEM),
        scratch_shapes=[
            vmem((2, 2, TILE, 256), F32),
            pltpu.SMEM((4, 2), jnp.int32),
            pltpu.SMEM((ITERS, 4, 2), jnp.int32),
            vmem((2, 2, TILE, 256), F32),
            vmem((ITERS, 16, 512, TILE), F32),
            vmem((ITERS, 8, 2, TILE, 256), F32),
            vmem((ITERS, 8, 2, TILE, 256), F32),
            vmem((512, 2048), BF16),
            vmem((512, 2048), BF16),
            vmem((2048, 256), BF16),
            vmem((2048, 256), BF16),
            vmem((2048, 256), BF16),
            vmem((2048, 256), BF16),
            vmem((ITERS, 2, 256, 256), F32),
            vmem((ITERS, 256, 256), F32),
            vmem((ITERS, 512, 256), F32),
            vmem((ITERS, 512, 256), F32),
            dma((4 + ITERS,)),
            dma((ITERS, 2, PARTS, 4)),
            dma((ITERS, PARTS)),
            dma((ITERS, max(1, len(BY_PARTNER)), 4)),
            dma((ITERS, 2, PARTS, 5)),
            dma((ITERS, PARTS + 2)),
            dma((3,)),
        ],
        compiler_params=pltpu.CompilerParams(
            collective_id=0, has_side_effects=True, vmem_limit_bytes=40 << 20
        ),
        name="sign_iterations",
    )(initial.reshape(2, 2, TILE, 256), pattern, filters)
    return out.reshape(512, TILE)


def solution(mesh):
    return jax.shard_map(
        on_device,
        mesh=mesh,
        in_specs=(P("row", "col"), P("row", "col"), P(None, "row", "col")),
        out_specs=P("row", ("col", "layer")),
        check_vma=False,
    )
```

time: 130 us -> 122 us (0.938)
  Pallas kernels: 128 us -> 119 us
    pallas_call x1, Pallas kernels: 128 us -> 119 us  [on_device(): pl.pallas_call(kernel, out_shape=jax.ShapeDtypeStruct((2, 2, TILE, TILE),...]
where the time goes in v3:
time: 122 us
  Pallas kernels  119 us (98%)
  local copies, waits for them, and re-layouts  2.63 us (2%)
    pallas_call x1, Pallas kernels, on_device(): pl.pallas_call(kernel, out_shape=jax.ShapeDtypeStruct((2, 2, TILE, TILE),...  119 us
    unnamed x7, local copies, waits for them, and re-layouts  2.63 us

profile of v3, /device:TPU:1, one launch (start us, length us, event | category | flops | bytes accessed | tf_op | source)
XLA Modules:
  0.0 122.1 jit_solution(13577202639990066880)
XLA Ops:
  0.0 0.0 copy-start.1
  0.0 0.8 copy.4.pattern_in
  0.8 0.0 copy-done.1
  0.8 0.1 copy.5.filters_in
  0.9 0.0 copy-start
  0.9 1.0 copy-done
  1.9 119.4 %sign_iterations.1 = f32[2,2,128,128]{3,2,1,0:T(8,128)S(1)} custom-call(f32[2,2,128,256]{3,2,1,0:T(8,128)S(1)} %bitcast.3, s32[4,2]{1,0:T(4,128)S(1)} %copy.4.pattern_in, s32[2,4,2]{2,1,0:T(4,128)S(1)} %copy.5.filters_in), custom_call_target="tpu_custom_call" | custom-call | tf_op jit(solution)/shard_map/sign_iterations/pallas_call | solution.py:342
  121.4 0.7 copy.7
Async XLA Ops:
  0.0 0.8 copy-start.1
  0.9 1.0 copy-start

commit v4 on v3

--- a/solution.py
+++ b/solution.py
@@ -13,28 +13,28 @@
 STARTS = tuple(sum(SIZES[:k]) for k in range(PARTS))
 F32 = jnp.float32
 BF16 = jnp.bfloat16
-BY_PARTNER = (1,)
+BY_PARTNER = (1, 3)
 FAR_BY_MATE = "S"
-STRAIGHT = (4,)
+STRAIGHT = {"B": (), "S": (4,)}
 STEPS = [
-    ("ox", 0), ("zb", 1), ("y", 0), ("ox", 1), ("zb", 3), ("bg", 4), ("y", 3), ("zb", 2), ("y", 4), ("zb", 0),
-    ("bg", 2), ("bg", 3), ("bg", 0), ("yb", 0), ("gm", "B", 4), ("y", 1), ("y", 2), ("bg", 1), ("gn", "B", 4, 0),
-    ("z", 0, 3, 1), ("z", 0, 1, 1), ("gn", "B", 2, 0), ("z", 0, 0, 1), ("gm", "B", 2), ("gm", "B", 3), ("yb", 3),
-    ("yb", 4), ("z", 1, 0, 1), ("z", 0, 1, 2), ("gn", "B", 1, 0), ("gm", "B", 0), ("yb", 2), ("gn", "B", 0, 0),
-    ("z", 1, 3, 1), ("gf", "B", 4, 0), ("z", 0, 0, 2), ("gn", "B", 3, 0), ("gm", "B", 1), ("z", 0, 1, 3),
-    ("gn", "B", 0, 1), ("yb", 1), ("gn", "B", 3, 1), ("gn", "B", 4, 1), ("z", 1, 0, 2), ("z", 1, 2, 1),
-    ("gn", "B", 1, 1), ("z", 1, 3, 2), ("z", 0, 3, 2), ("gn", "B", 2, 1), ("z", 0, 2, 1), ("z", 0, 1, 4),
-    ("gf", "B", 4, 1), ("gf", "B", 2, 0), ("z", 0, 0, 3), ("z", 1, 1, 1), ("z", 1, 0, 3), ("gf", "B", 3, 1),
-    ("gf", "B", 1, 0), ("z", 1, 1, 2), ("gf", "B", 0, 0), ("gf", "B", 1, 1), ("gf", "B", 3, 0), ("gf", "B", 2, 1),
-    ("z", 1, 1, 3), ("z", 1, 2, 2), ("z", 1, 3, 3), ("z", 1, 1, 4), ("zb", 4), ("gf", "B", 0, 1), ("sq", 1),
-    ("z", 0, 3, 3), ("z", 1, 4, 1), ("z", 0, 0, 4), ("z", 0, 2, 2), ("sr", 1), ("z", 1, 0, 4), ("sq", 0),
-    ("z", 0, 4, 1), ("z", 1, 3, 4), ("z", 1, 2, 3), ("sr", 0), ("z", 1, 4, 2), ("z", 0, 2, 3), ("gm", "S", 1),
-    ("z", 0, 3, 4), ("sq", 3), ("gn", "S", 1, 0), ("z", 0, 4, 2), ("gn", "S", 0, 0), ("gm", "S", 0), ("sr", 3),
-    ("z", 0, 2, 4), ("z", 1, 2, 4), ("sq", 2), ("z", 1, 4, 3), ("z", 0, 4, 3), ("sr", 2), ("gf", "S", 0, 0),
-    ("gf", "S", 1, 0), ("z", 0, 4, 4), ("gm", "S", 3), ("z", 1, 4, 4), ("sq", 4), ("gn", "S", 3, 0),
-    ("gn", "S", 2, 0), ("sr", 4), ("gn", "S", 1, 1), ("gn", "S", 0, 1), ("gf", "S", 3, 0), ("gn", "S", 3, 1),
-    ("gf", "S", 2, 0), ("gm", "S", 2), ("gd", "S", 4, 0), ("gf", "S", 1, 1), ("gf", "S", 0, 1), ("pr0", 0),
-    ("pr0", 1), ("gf", "S", 3, 1), ("gd", "S", 4, 1), ("gn", "S", 2, 1), ("gf", "S", 2, 1),
+    ("ox", 0), ("zb", 0), ("y", 0), ("zb", 1), ("ox", 1), ("bg", 1), ("bg", 0), ("bg", 3), ("zb", 3), ("zb", 2),
+    ("y", 2), ("yb", 0), ("z", 0, 0, 1), ("gm", "B", 1), ("bg", 2), ("z", 0, 3, 1), ("z", 0, 1, 1), ("gm", "B", 3),
+    ("gn", "B", 0, 0), ("gm", "B", 0), ("yb", 2), ("gn", "B", 1, 0), ("z", 1, 0, 1), ("bg", 4), ("gn", "B", 3, 0),
+    ("z", 0, 3, 2), ("z", 0, 0, 2), ("y", 1), ("gm", "B", 2), ("z", 0, 1, 2), ("z", 1, 2, 1), ("gn", "B", 2, 0),
+    ("gm", "B", 4), ("gn", "B", 0, 1), ("gn", "B", 4, 0), ("y", 3), ("y", 4), ("z", 1, 0, 2), ("gn", "B", 1, 1),
+    ("gf", "B", 3, 0), ("gn", "B", 2, 1), ("z", 0, 2, 1), ("z", 0, 1, 3), ("yb", 1), ("gn", "B", 4, 1),
+    ("gn", "B", 3, 1), ("gf", "B", 0, 1), ("z", 0, 0, 3), ("z", 1, 1, 1), ("z", 0, 3, 3), ("z", 1, 0, 3),
+    ("zb", 4), ("gf", "B", 0, 0), ("gf", "B", 2, 0), ("gf", "B", 1, 1), ("yb", 4), ("yb", 3), ("gf", "B", 1, 0),
+    ("gf", "B", 2, 1), ("z", 1, 2, 2), ("gf", "B", 4, 0), ("gf", "B", 4, 1), ("gf", "B", 3, 1), ("z", 1, 3, 1),
+    ("z", 0, 1, 4), ("z", 0, 0, 4), ("z", 0, 2, 2), ("z", 1, 1, 2), ("z", 0, 3, 4), ("z", 1, 1, 3), ("z", 1, 0, 4),
+    ("sq", 0), ("z", 1, 3, 2), ("z", 1, 4, 1), ("z", 0, 4, 1), ("z", 1, 1, 4), ("sr", 0), ("sq", 1),
+    ("z", 1, 2, 3), ("z", 0, 2, 3), ("sr", 1), ("z", 1, 3, 3), ("z", 1, 3, 4), ("z", 1, 4, 2), ("sq", 3),
+    ("gm", "S", 0), ("z", 0, 4, 2), ("gn", "S", 0, 0), ("sr", 3), ("z", 1, 2, 4), ("z", 0, 2, 4), ("sq", 2),
+    ("gn", "S", 1, 0), ("z", 1, 4, 3), ("sr", 2), ("z", 0, 4, 3), ("gf", "S", 0, 0), ("gm", "S", 3),
+    ("gm", "S", 1), ("gn", "S", 3, 0), ("z", 1, 4, 4), ("z", 0, 4, 4), ("sq", 4), ("gf", "S", 1, 0),
+    ("gn", "S", 2, 0), ("sr", 4), ("gn", "S", 1, 1), ("gf", "S", 1, 1), ("gn", "S", 0, 1), ("gn", "S", 3, 1),
+    ("gf", "S", 3, 0), ("gf", "S", 0, 1), ("gm", "S", 2), ("gf", "S", 2, 0), ("gd", "S", 4, 0), ("pr0", 1),
+    ("pr0", 0), ("gf", "S", 3, 1), ("gd", "S", 4, 1), ("gn", "S", 2, 1), ("gf", "S", 2, 1),
 ]
 
 
@@ -73,7 +73,7 @@
 
     barrier = pltpu.get_barrier_semaphore()
     neighbours = (at_x(1), at_x(-1), at_z(1), at_z(-1), mate_lo, mate_hi, sibling)
-    if STRAIGHT:
+    if any(STRAIGHT.values()):
         neighbours += (at_x(2), mate_x(1), mate_x(-1), mate_x(2))
     for device in neighbours:
         pl.semaphore_signal(barrier, inc=1, device_id=device, device_id_type=MESH)
@@ -143,7 +143,7 @@
 
     def g_copy(it, kind, part, what):
         way = (part + what - 5) % 2
-        if kind == "S" and part in STRAIGHT:
+        if part in STRAIGHT[kind]:
             slot = row
             device = (mate_lo, at_x(1), at_x(-1), mate_x(1), mate_x(-1), at_x(2), mate_x(2))[what]
         elif what == 0:
@@ -158,7 +158,7 @@
         return remote(piece, piece, sent.at[1 + "BS".index(kind)], g_sem(it, kind, part, what), device)
 
     def g_sem(it, kind, part, what):
-        straight_on = kind == "S" and part in STRAIGHT
+        straight_on = part in STRAIGHT[kind]
         return g_recv.at[it, "BS".index(kind), part, int(what > 2) if straight_on else (0, 1, 1, 2, 2, 3, 4)[what]]
 
     def g_wait(it, kind, part, what, count):
@@ -189,9 +189,12 @@
         for side in range(2):
             rows = pl.ds(2 * STARTS[part] + side * SIZES[part], SIZES[part])
             a_in[it, col, rows] = own[half_of(part), side, span(part), mine]
-        split_a(it, part, col)
         b_in[it, row, half_of(part), span(part)] = own[half_of(part), layer, span(part)]
-        split_b(it, "B", part, row)
+
+    def own_parts(it, half):
+        for k in range(PARTS):
+            if half_of(k) == half:
+                own_part(it, k)
 
     def iteration(it, update_before):
         def y_begin(k):
@@ -200,6 +203,7 @@
         def z_begin(k):
             z_copy(it, 0, k, 0, 0).start()
             z_copy(it, 0, k, 1, 0).start()
+            split_a(it, k, col)
 
         def y_arrives(k):
             y_copy(it, k).wait_recv()
@@ -223,8 +227,9 @@
                 split_a(it, k, z_slot(group, way, depth))
 
         def column_begin(part):
-            for what in range(3):
+            for what in range(7 if part in STRAIGHT["B"] else 3):
                 g_copy(it, "B", part, what).start()
+            split_b(it, "B", part, row)
 
         def straight(kind, part, far):
             whats = (3, 4, 5, 6) if far else (0, 1, 2)
@@ -263,7 +268,7 @@
             e_copy(it, part).wait_recv()
             value = sq_part[it, layer, rows_of(part)] + sq_from[it, rows_of(part)]
             s_in[it, row, half_of(part), span(part)] = tile_mask(filters, (it, 2 * half_of(part) + layer), value)
-            for what in range(7 if part in STRAIGHT else 3):
+            for what in range(7 if part in STRAIGHT["S"] else 3):
                 g_copy(it, "S", part, what).start()
             split_b(it, "S", part, row)
 
@@ -298,12 +303,7 @@
         def own_half(part):
             if update_before is not None:
                 update_before(part)
-            else:
-                for side in range(2):
-                    own[part, side] = tile_mask(pattern, (2 * part + side,), raw[part, side])
-            for k in range(PARTS):
-                if half_of(k) == part:
-                    own_part(it, k)
+                own_parts(it, part)
 
         run = {
             "ox": own_half,
@@ -325,6 +325,10 @@
         copy.start()
     for copy in fetch:
         copy.wait()
+    for half in range(2):
+        for side in range(2):
+            own[half, side] = tile_mask(pattern, (2 * half + side,), raw[half, side])
+        own_parts(0, half)
     pl.semaphore_wait(barrier, len(neighbours))
     before = None
     for it in range(ITERS):

time: 122 us -> 119 us (0.975)
  Pallas kernels: 119 us -> 116 us
    pallas_call x1, Pallas kernels: 119 us -> 116 us  [on_device(): pl.pallas_call(kernel, out_shape=jax.ShapeDtypeStruct((2, 2, TILE, TILE),...]
where the time goes in v4:
time: 119 us
  Pallas kernels  116 us (97%)
  local copies, waits for them, and re-layouts  2.63 us (2%)
    pallas_call x1, Pallas kernels, on_device(): pl.pallas_call(kernel, out_shape=jax.ShapeDtypeStruct((2, 2, TILE, TILE),...  116 us
    unnamed x7, local copies, waits for them, and re-layouts  2.63 us

profile of v4, /device:TPU:1, one launch (start us, length us, event | category | flops | bytes accessed | tf_op | source)
XLA Modules:
  0.0 118.6 jit_solution(10339924946856596363)
XLA Ops:
  0.0 0.0 copy-start.1
  0.0 0.8 copy.4.pattern_in
  0.8 0.0 copy-done.1
  0.8 0.1 copy.5.filters_in
  0.9 0.0 copy-start
  0.9 1.0 copy-done
  1.9 115.9 %sign_iterations.1 = f32[2,2,128,128]{3,2,1,0:T(8,128)S(1)} custom-call(f32[2,2,128,256]{3,2,1,0:T(8,128)S(1)} %bitcast.3, s32[4,2]{1,0:T(4,128)S(1)} %copy.4.pattern_in, s32[2,4,2]{2,1,0:T(4,128)S(1)} %copy.5.filters_in), custom_call_target="tpu_custom_call" | custom-call | tf_op jit(solution)/shard_map/sign_iterations/pallas_call | solution.py:346
  117.9 0.7 copy.7
Async XLA Ops:
  0.0 0.8 copy-start.1
  0.9 1.0 copy-start

commit v5 on v4

--- a/solution.py
+++ b/solution.py
@@ -317,10 +317,9 @@
         product(False, 1)
         return update
 
-    fetch = [
-        pltpu.make_async_copy(src, dst, in_sem.at[index])
-        for index, (src, dst) in enumerate(((initial, raw), (pattern_in, pattern), (filters_in, filters)))
-    ]
+    parts = [(initial.at[pl.ds(tile * TILE, TILE)], raw.at[tile // 2, tile % 2]) for tile in range(4)]
+    parts += [(pattern_in, pattern), (filters_in, filters)]
+    fetch = [pltpu.make_async_copy(src, dst, in_sem.at[index]) for index, (src, dst) in enumerate(parts)]
     for copy in fetch:
         copy.start()
     for copy in fetch:
@@ -376,13 +375,13 @@
             dma((ITERS, max(1, len(BY_PARTNER)), 4)),
             dma((ITERS, 2, PARTS, 5)),
             dma((ITERS, PARTS + 2)),
-            dma((3,)),
+            dma((6,)),
         ],
         compiler_params=pltpu.CompilerParams(
-            collective_id=0, has_side_effects=True, vmem_limit_bytes=40 << 20
+            collective_id=0, has_side_effects=True, vmem_limit_bytes=54600 << 10
         ),
         name="sign_iterations",
-    )(initial.reshape(2, 2, TILE, 256), pattern, filters)
+    )(initial, pattern, filters)
     return out.reshape(512, TILE)
 
 

time: 119 us -> 118 us (level)
    unnamed x7 -> x5, local copies, waits for them, and re-layouts: 2.63 us -> 1.58 us
where the time goes in v5:
time: 118 us
  Pallas kernels  116 us (98%)
  local copies, waits for them, and re-layouts  1.58 us (1%)
    pallas_call x1, Pallas kernels, on_device(): pl.pallas_call(kernel, out_shape=jax.ShapeDtypeStruct((2, 2, TILE, TILE),...  116 us

profile of v5, /device:TPU:1, one launch (start us, length us, event | category | flops | bytes accessed | tf_op | source)
XLA Modules:
  0.0 117.7 jit_solution(2715122698600716229)
XLA Ops:
  0.0 0.0 copy-start
  0.0 0.8 copy.4.pattern_in
  0.8 0.0 copy-done
  0.8 0.1 copy.5.filters_in
  0.9 116.1 %sign_iterations.1 = f32[2,2,128,128]{3,2,1,0:T(8,128)S(1)} custom-call(f32[512,256]{1,0:T(8,128)} %initial.1, s32[4,2]{1,0:T(4,128)S(1)} %copy.4.pattern_in, s32[2,4,2]{2,1,0:T(4,128)S(1)} %copy.5.filters_in), custom_call_target="tpu_custom_call" | custom-call | tf_op jit(solution)/shard_map/sign_iterations/pallas_call | solution.py:345
  117.0 0.7 copy.7
Async XLA Ops:
  0.0 0.8 copy-start

commit v6 on v5

--- a/solution.py
+++ b/solution.py
@@ -87,7 +87,7 @@
     def tile_mask(ref, index, value):
         parts = []
         for ct in range(2):
-            parts.append(value[:, ct * TILE : (ct + 1) * TILE] * ref[(*index, ct)].astype(F32))
+            parts.append(value[:, ct * TILE : (ct + 1) * TILE] * ref[(*index[:-1], ct, index[-1])].astype(F32))
         return jnp.concatenate(parts, axis=1)
 
     def remote(src, dst, send, recv, device):
@@ -296,7 +296,7 @@
                         own[place] = 1.5 * own[place] - 0.5 * value
                     else:
                         value = (pr_part[it, rows, mine] + pr_from[it, rows, mine]) * filters[
-                            it, 2 * part + side, layer
+                            it, layer, 2 * part + side
                         ].astype(F32)
                         out[place] = 1.5 * own[(*place, mine)] - 0.5 * value
 
@@ -353,8 +353,8 @@
         out_specs=pl.BlockSpec(memory_space=pltpu.VMEM),
         scratch_shapes=[
             vmem((2, 2, TILE, 256), F32),
-            pltpu.SMEM((4, 2), jnp.int32),
-            pltpu.SMEM((ITERS, 4, 2), jnp.int32),
+            pltpu.SMEM((2, 4), jnp.int32),
+            pltpu.SMEM((ITERS, 2, 4), jnp.int32),
             vmem((2, 2, TILE, 256), F32),
             vmem((ITERS, 16, 512, TILE), F32),
             vmem((ITERS, 8, 2, TILE, 256), F32),
@@ -381,7 +381,7 @@
             collective_id=0, has_side_effects=True, vmem_limit_bytes=54600 << 10
         ),
         name="sign_iterations",
-    )(initial, pattern, filters)
+    )(initial, pattern.T, filters.swapaxes(1, 2))
     return out.reshape(512, TILE)
 
 

time: 118 us -> 117 us (level)
  no operation moved by 1% of the time
where the time goes in v6:
time: 117 us
  Pallas kernels  116 us (99%)
  local copies, waits for them, and re-layouts  1.4 us (1%)
    pallas_call x1, Pallas kernels, on_device(): pl.pallas_call(kernel, out_shape=jax.ShapeDtypeStruct((2, 2, TILE, TILE),...  116 us

profile of v6, /device:TPU:1, one launch (start us, length us, event | category | flops | bytes accessed | tf_op | source)
XLA Modules:
  0.0 117.4 jit_solution(4298895508385993133)
XLA Ops:
  0.0 0.0 copy-start
  0.0 0.0 copy-start.1
  0.0 0.7 copy-done
  0.7 0.0 copy-done.1
  0.7 116.0 %sign_iterations.1 = f32[2,2,128,128]{3,2,1,0:T(8,128)S(1)} custom-call(f32[512,256]{1,0:T(8,128)} %initial.1, s32[2,4]{1,0:T(2,128)S(1)} %bitcast.5, s32[2,2,4]{2,1,0:T(2,128)S(1)} %bitcast.4), custom_call_target="tpu_custom_call" | custom-call | tf_op jit(solution)/shard_map/sign_iterations/pallas_call | solution.py:345
  116.7 0.7 copy.5
Async XLA Ops:
  0.0 0.7 copy-start
  0.0 0.7 copy-start.1

commit v7 on v6

--- a/solution.py
+++ b/solution.py
@@ -53,7 +53,7 @@
 def kernel(
     initial, pattern_in, filters_in, out,
     raw, pattern, filters, own, a_in, b_in, s_in, a_hi, a_lo, b_hi, b_lo, s_hi, s_lo, sq_part, sq_from, pr_part, pr_from,
-    sent, a_recv, y_recv, p_recv, g_recv, e_recv, in_sem,
+    sent, a_recv, y_recv, g_recv, e_recv, in_sem,
 ):
     row, col, layer = lax.axis_index("row"), lax.axis_index("col"), lax.axis_index("layer")
     x, y_lo = lax.rem(row, 4), row // 4
@@ -119,7 +119,7 @@
 
     def p_copy(it, k, way, depth):
         piece = a_piece(it, k, z_slot(0, way, depth))
-        return remote(piece, piece, sent.at[0], p_recv.at[it, BY_PARTNER.index(k), depth - 1], mate_hi)
+        return remote(piece, piece, sent.at[0], a_recv.at[it, 1, k, depth - 1], mate_hi)
 
     def split_a(it, k, slot):
         columns = pl.ds(pl.multiple_of(lax.rem(slot, 2) * 1024 + slot // 2 * TILE, TILE), TILE)
@@ -215,7 +215,7 @@
         def z_arrives(group, k, depth):
             ways = [way for way in range(2) if depth < 4 or way == far_way(group, k)]
             if group == 1 and k in BY_PARTNER:
-                a_wait(it, k, depth, p_recv.at[it, BY_PARTNER.index(k), depth - 1])
+                a_wait(it, k, depth, a_recv.at[it, 1, k, depth - 1])
             else:
                 a_wait(it, k, depth, a_recv.at[it, group, k, depth - 1])
                 for way in ways:
@@ -372,7 +372,6 @@
             dma((4 + ITERS,)),
             dma((ITERS, 2, PARTS, 4)),
             dma((ITERS, PARTS)),
-            dma((ITERS, max(1, len(BY_PARTNER)), 4)),
             dma((ITERS, 2, PARTS, 5)),
             dma((ITERS, PARTS + 2)),
             dma((6,)),

time: 117 us -> 117 us (level)
  no operation moved by 1% of the time
where the time goes in v7:
time: 117 us
  Pallas kernels  116 us (99%)
  local copies, waits for them, and re-layouts  1.4 us (1%)
    pallas_call x1, Pallas kernels, on_device(): pl.pallas_call(kernel, out_shape=jax.ShapeDtypeStruct((2, 2, TILE, TILE),...  116 us

profile of v7, /device:TPU:1, one launch (start us, length us, event | category | flops | bytes accessed | tf_op | source)
XLA Modules:
  0.0 117.2 jit_solution(7707654448564686514)
XLA Ops:
  0.0 0.0 copy-start
  0.0 0.0 copy-start.1
  0.0 0.7 copy-done
  0.7 0.0 copy-done.1
  0.7 115.8 %sign_iterations.1 = f32[2,2,128,128]{3,2,1,0:T(8,128)S(1)} custom-call(f32[512,256]{1,0:T(8,128)} %initial.1, s32[2,4]{1,0:T(2,128)S(1)} %bitcast.5, s32[2,2,4]{2,1,0:T(2,128)S(1)} %bitcast.4), custom_call_target="tpu_custom_call" | custom-call | tf_op jit(solution)/shard_map/sign_iterations/pallas_call | solution.py:345
  116.5 0.7 copy.5
Async XLA Ops:
  0.0 0.7 copy-start
  0.0 0.7 copy-start.1
